TPU v7x, 128 devices: a whole 4x4x4 slice. The times are simulated.
128 devices in a mesh: mem: 16 (over z, x), slab: 8 (over y, core).
Axes of the slice: x: 4, y: 4, z: 4, core: 2. Of those that a mesh axis runs over, the one named last changes fastest.
Arguments:
- pressure: float32 [128, 256, 4096], P('mem', 'slab'), may hold values from 0.5 to 3
- content: float32 [128, 256, 4096], P('mem', 'slab'), may hold values from 0.5 to 3
- diffusivity: float32 [256, 4096], P('slab'), may hold values from 0.05 to 1
- langmuir_pressure: float32 [256, 4096], P('slab'), may hold values from 0.5 to 4
- langmuir_volume: float32 [256, 4096], P('slab'), may hold values from 1 to 3
- desorb_rate: float32 [256, 4096], P('slab'), may hold values from 0.02 to 0.5
- observed_cell: int32 [64, 128, 16], P('slab', 'mem'), may hold values from 0 to 127
- observed_value: float32 [64, 128, 16], P('slab', 'mem'), may hold values from 0.5 to 3.5
- error_weight: float32 [64, 128, 16], P('slab', 'mem'), may hold values from 0.25 to 2.5
- observed_count: int32 [64, 128], P('slab', 'mem'), may hold values from 1 to 16, as said below
- neighbour: int32 [64, 128, 4], P('slab', 'mem'), may hold values from 0 to 8, as said below
Outputs:
- analysis: float32 [128, 256, 4096], P(None, 'slab', 'mem')
- gas_content: float32 [128, 256, 4096], P('mem', 'slab')
Inputs may be any that keep to these rules, and one draw needn't show every extreme that they name: `observed_cell`: the slot's cell within its block, row * 32 + column. Some block has 16 live slots and some block has 1; slots j < observed_count are live. `neighbour`: A block's 4 codes are distinct; code q names the block (q // 3 - 1, q % 3 - 1) away, 4 the block itself.
All inputs are finite; a program needn't handle non-finite values.
Results may differ from a plain program's by a relative error of at most 0.0001.
Values sent between devices are 32-bit elements; how exact they have to be, the bound alone decides.
A program may use at most 192 MiB of HBM per device.

v0:
```python
import math

import jax
import jax.numpy as jnp
from jax import lax
from jax.experimental import pallas as pl
from jax.experimental.pallas import tpu as pltpu
from jax.sharding import PartitionSpec as P

MEMBERS = 128
STEPS = 4
BR = 4
BC = 32
OBS_MAX = 16
NBR = 4
NS_ITERS = 7

PEERS = 16
SLABS = 8
OWN = 8
ROWS = 32
COLS = 4096
TILES = 32
PAD_ROWS = 48
BLOCKS = 64
SIDE = 8
PAIRS = 8
PARTS = 4
HALF = NBR * OBS_MAX

inflation = 1.1
ridge = (MEMBERS - 1) / inflation
member_root = math.sqrt(MEMBERS - 1)
side_weight = math.exp(-0.25)
corner_weight = math.exp(-0.5)
mesh_ids = pl.DeviceIdType.MESH

ways = (
    (1, 0), (3, 0), (2, 2), (0, 2), (2, 0), (1, 1), (3, 3), (1, 3), (3, 1), (2, 1), (1, 2),
    (2, 3), (3, 2), (0, 1), (0, 3),
)


def split(value):
    head = value.astype(jnp.bfloat16)
    return head, (value - head.astype(jnp.float32)).astype(jnp.bfloat16)


def product(left, head, tail):
    left_head, left_tail = split(left)
    both = jnp.concatenate([head, tail], axis=1)
    result = jnp.dot(
        jnp.concatenate([left_head, left_tail], axis=1),
        jnp.concatenate([both, both], axis=0),
        preferred_element_type=jnp.float32,
    )
    columns = head.shape[1]
    return result[:, :columns] + result[:, columns:]


def pair_product(left, right):
    same = (lax.broadcasted_iota(jnp.int32, (128, 128), 0) < HALF) == (
        lax.broadcasted_iota(jnp.int32, (128, 128), 1) < HALF
    )
    head, tail = (
        jnp.where(same, jnp.concatenate([part, part], axis=0), jnp.zeros((128, 128), jnp.bfloat16))
        for part in split(right)
    )
    return product(left, head, tail)


def swap_groups(rows):
    group = lax.broadcasted_iota(jnp.int32, (8, 128), 1) // BC
    even = group % 2 == 0
    low = group < 2
    near = [None] * 4
    for i in (0, 2):
        near[i] = jnp.where(even, rows[i], pltpu.roll(rows[i + 1], BC, 1))
        near[i + 1] = jnp.where(even, pltpu.roll(rows[i], 128 - BC, 1), rows[i + 1])
    out = [None] * 4
    for i in (0, 1):
        out[i] = jnp.where(low, near[i], pltpu.roll(near[i + 2], 64, 1))
        out[i + 2] = jnp.where(low, pltpu.roll(near[i], 64, 1), near[i + 2])
    return out


def assimilate_kernel(
    p_in, c_in, d_in, lp_in, lv_in, rate_in, cell_in, value_in, error_in, count_in, neighbour,
    analysis, c_out,
    p, p_other, c, c_other, lp, lv, rate, dif, dif_top, dif_low, keep, k_up, k_down, k_left, k_right,
    out_up, out_down, in_top, in_low, send,
    cells, values, roots, all_cells, obs_send, obs_in, obs_pad,
    rows_z, innov_z, now_x, now_m, now_d, weights_now, gathered, lines,
    load_sem, p_sem, dif_send, dif_recv, halo_send, halo_recv, send_sem, recv_sem, own_sem, c_sem,
    cell_send, cell_recv, obs_send_sem, obs_recv_sem, side_send, side_recv, out_sem,
):
    mem = lax.axis_index("mem")
    slab = lax.axis_index("slab")
    above = lax.rem(slab + SLABS - 1, SLABS)
    below = lax.rem(slab + 1, SLABS)

    def load_p(tile):
        return pltpu.make_async_copy(
            p_in.at[:, :, pl.ds(pl.multiple_of(tile * 128, 128), 128)],
            p.at[tile + 1, :, pl.ds(8, ROWS), :],
            p_sem.at[tile],
        )

    loads = [
        pltpu.make_async_copy(src, dst, load_sem.at[i])
        for i, (src, dst) in enumerate(
            ((d_in, dif), (lp_in, lp), (lv_in, lv), (rate_in, rate), (c_in, c))
        )
    ]
    for load in loads[:1]:
        load.start()

    @pl.loop(0, TILES)
    def _(tile):
        load_p(tile).start()

    for load in loads[1:]:
        load.start()

    lane = lax.broadcasted_iota(jnp.int32, (8, 128), 1)
    line = lax.broadcasted_iota(jnp.int32, (8, 128), 0)
    slot_group = lane // OBS_MAX

    def lay_out(piece_of):
        out = piece_of(0)
        for b in range(1, SIDE):
            out = jnp.where(slot_group == b, piece_of(b), out)
        return out

    def slots_of(ref):
        return lay_out(lambda b: jnp.concatenate([ref[:, b, :]] * SIDE, axis=1))

    cells[...] = slots_of(cell_in)
    values[...] = slots_of(value_in)
    counts = lay_out(lambda b: jnp.broadcast_to(count_in[:, b : b + 1], (SIDE, 128)))
    live = lax.rem(lane, OBS_MAX) < counts
    roots[...] = jnp.where(live, jnp.sqrt(slots_of(error_in)), 0.0)

    barrier = pltpu.get_barrier_semaphore()

    @pl.loop(1, PEERS)
    def _(i):
        pl.semaphore_signal(
            barrier, inc=1, device_id=(lax.rem(mem + i, PEERS), slab),
            device_id_type=pl.DeviceIdType.MESH,
        )

    for other in (above, below):
        pl.semaphore_signal(
            barrier, inc=1, device_id=(mem, other), device_id_type=pl.DeviceIdType.MESH
        )

    zero = jnp.zeros((8, 128), jnp.float32)
    for field in (p, p_other):
        for tile in (0, TILES + 1):
            for m in range(OWN):
                for i in range(PAD_ROWS // 8):
                    field[tile, m, i * 8 : i * 8 + 8, :] = zero

    pl.semaphore_wait(barrier, PEERS + 1)

    def dif_copy(i, src, dst, other):
        return pltpu.make_async_remote_copy(
            src_ref=src, dst_ref=dst, send_sem=dif_send.at[i], recv_sem=dif_recv.at[i],
            device_id=(mem, other), device_id_type=pl.DeviceIdType.MESH,
        )

    def cell_copy(i):
        return pltpu.make_async_remote_copy(
            src_ref=cells, dst_ref=all_cells.at[mem],
            send_sem=cell_send.at[i], recv_sem=cell_recv.at[i],
            device_id=(lax.rem(mem + i, PEERS), slab), device_id_type=mesh_ids,
        )

    @pl.loop(1, PEERS)
    def _(i):
        cell_copy(i).start()

    all_cells[mem] = cells[...]

    dif_copies = [
        dif_copy(0, d_in.at[pl.ds(24, 8)], dif_top, below),
        dif_copy(1, d_in.at[pl.ds(0, 8)], dif_low, above),
    ]
    for copy in dif_copies:
        copy.start()

    def halo_copy(step, i):
        src, dst, other = ((out_down, in_top, below), (out_up, in_low, above))[i]
        return pltpu.make_async_remote_copy(
            src_ref=src.at[step], dst_ref=dst.at[step],
            send_sem=halo_send.at[step, i], recv_sem=halo_recv.at[step, i],
            device_id=(mem, other), device_id_type=pl.DeviceIdType.MESH,
        )

    flat, flat_other = (
        field.reshape(TILES + 2, OWN * PAD_ROWS, 128) for field in (p, p_other)
    )

    def send_halo(step, source):

        @pl.loop(0, TILES)
        def _(tile):
            out_up[step, tile] = source[tile + 1, pl.ds(8, OWN, stride=PAD_ROWS), :]
            out_down[step, tile] = source[
                tile + 1, pl.ds(7 + ROWS, OWN, stride=PAD_ROWS), :
            ]

        for i in range(2):
            halo_copy(step, i).start()

    @pl.loop(0, TILES)
    def _(tile):
        load_p(tile).wait()

    send_halo(0, flat)

    for load in loads:
        load.wait()
    for copy in dif_copies:
        copy.wait()

    first, last = lane == 0, lane == 127
    at_top, at_low = slab == 0, slab == SLABS - 1

    @pl.loop(0, TILES)
    def _(tile):
        here = pl.ds(pl.multiple_of(tile * 128, 128), 128)
        left = pl.ds(pl.multiple_of(jnp.maximum(tile - 1, 0) * 128, 128), 128)
        right = pl.ds(pl.multiple_of(jnp.minimum(tile + 1, TILES - 1) * 128, 128), 128)
        top_row = jnp.where(at_top, 0.0, dif_top[:, here])
        low_row = jnp.where(at_low, 0.0, dif_low[:, here])
        mids = [dif[i * 8 : i * 8 + 8, here] for i in range(4)]
        column = [top_row, *mids, low_row]
        for i in range(4):
            rows = slice(i * 8, i * 8 + 8)
            mid = mids[i]
            up = jnp.where(line == 0, pltpu.roll(column[i], 1, 0), pltpu.roll(mid, 1, 0))
            down = jnp.where(line == 7, pltpu.roll(column[i + 2], 7, 0), pltpu.roll(mid, 7, 0))
            next_left = jnp.where(tile == 0, 0.0, dif[rows, left])
            next_right = jnp.where(tile == TILES - 1, 0.0, dif[rows, right])
            west = jnp.where(first, pltpu.roll(next_left, 1, 1), pltpu.roll(mid, 1, 1))
            east = jnp.where(last, pltpu.roll(next_right, 127, 1), pltpu.roll(mid, 127, 1))
            sides = [0.1 * (mid + side) for side in (up, down, west, east)]
            for ref, side in zip((k_up, k_down, k_left, k_right), sides):
                ref[rows, here] = side
            keep[rows, here] = 1.0 - ((sides[0] + sides[1]) + (sides[2] + sides[3]))
            lv[rows, here] = lv[rows, here] * rate[rows, here]

    wide = 4

    def advance(now, content_now, later, content_later, row_tiles):

        @pl.loop(0, TILES // wide)
        def _(group):
            for row_tile in row_tiles:
                rows = slice(row_tile * 8, row_tile * 8 + 8)
                base = 8 + row_tile * 8
                heres = [
                    pl.ds(pl.multiple_of((group * wide + j) * 128, 128), 128) for j in range(wide)
                ]
                weights = [
                    [ref[rows, here] for ref in (keep, k_up, k_down, k_left, k_right, lp, lv, rate)]
                    for here in heres
                ]
                for m in range(OWN):
                    mids = [
                        now[group * wide + j, m, base : base + 8, :] for j in range(wide + 2)
                    ]
                    to_right = [pltpu.roll(mids[j], 1, 1) for j in range(wide + 1)]
                    to_left = [None] + [pltpu.roll(mids[j], 127, 1) for j in range(1, wide + 2)]
                    for j in range(wide):
                        keep_w, up_w, down_w, left_w, right_w, lp_w, lv_w, rate_w = weights[j]
                        tile = group * wide + j + 1
                        mid = mids[j + 1]
                        up = now[tile, m, base - 1 : base + 7, :]
                        down = now[tile, m, base + 1 : base + 9, :]
                        west = jnp.where(first, to_right[j], to_right[j + 1])
                        east = jnp.where(last, to_left[j + 2], to_left[j + 1])
                        content = content_now[m, rows, heres[j]]
                        inverse = pltpu.reciprocal(lp_w + jnp.abs(mid), approx=True)
                        release = rate_w * content - (lv_w * mid) * inverse
                        flow = (up_w * up + down_w * down) + (left_w * west + right_w * east)
                        later[tile, m, base : base + 8, :] = (
                            keep_w * mid + flow + release
                        )
                        content_later[m, rows, heres[j]] = content - release

    def one_step(step, now, content_now, later, content_later, flat_now, flat_later, more):
        advance(now, content_now, later, content_later, (1, 2))
        for i in range(2):
            halo_copy(step, i).wait()

        @pl.loop(0, TILES)
        def _(tile):
            top = jnp.where(at_top, 0.0, in_top[step, tile])
            low = jnp.where(at_low, 0.0, in_low[step, tile])
            flat_now[tile + 1, pl.ds(7, OWN, stride=PAD_ROWS), :] = top
            flat_now[tile + 1, pl.ds(8 + ROWS, OWN, stride=PAD_ROWS), :] = low

        advance(now, content_now, later, content_later, (0, 3))

        @pl.when(more)
        def _():
            send_halo(step + 1, flat_later)

    @pl.loop(0, STEPS // 2)
    def _(pair):
        one_step(2 * pair, p, c, p_other, c_other, flat, flat_other, True)
        one_step(2 * pair + 1, p_other, c_other, p, c, flat_other, flat, pair < STEPS // 2 - 1)

    store_c = pltpu.make_async_copy(c, c_out, c_sem)
    store_c.start()

    @pl.loop(1, PEERS)
    def _(i):
        cell_copy(i).wait()

    def to_blocks(target):
        for a in range(SIDE):
            index = jnp.broadcast_to(all_cells[target, a : a + 1, :], (OWN, 128))
            observed = jnp.zeros((OWN, 128), jnp.float32)
            for j in range(2):
                lines = [
                    flat[target * 2 + j + 1, pl.ds(8 + a * BR + r, OWN, stride=PAD_ROWS), :]
                    for r in range(BR)
                ]
                blocks = swap_groups(lines)
                for b in range(4):
                    send[target, a * SIDE + j * 4 + b] = blocks[b]
                    picked = jnp.take_along_axis(blocks[b], index, axis=1)
                    observed = jnp.where(slot_group == j * 4 + b, picked, observed)
            obs_send[target, a] = observed

    mine = pl.ds(pl.multiple_of(mem * OWN, OWN), OWN)

    def obs_copy(i):
        target = lax.rem(mem + i, PEERS)
        return pltpu.make_async_remote_copy(
            src_ref=obs_send.at[target], dst_ref=obs_in.at[:, mine, :],
            send_sem=obs_send_sem.at[i], recv_sem=obs_recv_sem.at[i],
            device_id=(target, slab), device_id_type=mesh_ids,
        )

    def block_copy(part, i):
        way = ways[i]
        target = lax.rem(mem // 4 + way[0], 4) * 4 + lax.rem(mem + way[1], 4)
        blocks = pl.ds(part * 2 * SIDE, 2 * SIDE)
        return pltpu.make_async_remote_copy(
            src_ref=send.at[target, blocks], dst_ref=gathered.at[blocks, mine, :],
            send_sem=send_sem.at[part, i], recv_sem=recv_sem.at[part, i],
            device_id=(target, slab), device_id_type=mesh_ids,
        )

    @pl.loop(1, PEERS)
    def _(i):
        to_blocks(lax.rem(mem + i, PEERS))
        obs_copy(i).start()

    to_blocks(mem)
    for i in range(len(ways)):
        block_copy(0, i).start()
    own = pltpu.make_async_copy(send.at[mem], gathered.at[:, mine, :], own_sem.at[0])
    own.start()
    own_obs = pltpu.make_async_copy(obs_send.at[mem], obs_in.at[:, mine, :], own_sem.at[1])
    own_obs.start()
    own_obs.wait()

    @pl.loop(1, PEERS)
    def _(i):
        obs_copy(i).wait()

    @pl.loop(0, SIDE)
    def _(a):
        seen = obs_in[a]
        centre = jnp.mean(seen, axis=0, keepdims=True)
        root = roots[pl.ds(a, 1), :]
        spread = ((seen - centre) * root).T
        innovation = jnp.broadcast_to((values[pl.ds(a, 1), :] - centre) * root, (128, 128)).T
        for b in range(SIDE):
            obs_pad[a + 1, b + 1, 0:OBS_MAX, :] = spread[b * OBS_MAX : (b + 1) * OBS_MAX]
            obs_pad[a + 1, b + 1, OBS_MAX:, :] = innovation[b * OBS_MAX : (b + 1) * OBS_MAX]

    def side_copy(i):
        src, dst, device = (
            (obs_pad.at[1:9, 8], obs_pad.at[1:9, 0], (lax.rem(mem + 1, PEERS), slab)),
            (obs_pad.at[1:9, 1], obs_pad.at[1:9, 9], (lax.rem(mem + PEERS - 1, PEERS), slab)),
            (obs_pad.at[8], obs_pad.at[0], (mem, below)),
            (obs_pad.at[1], obs_pad.at[9], (mem, above)),
        )[i]
        return pltpu.make_async_remote_copy(
            src_ref=src, dst_ref=dst, send_sem=side_send.at[i], recv_sem=side_recv.at[i],
            device_id=device, device_id_type=mesh_ids,
        )

    blank = jnp.zeros((2 * OBS_MAX, 128), jnp.float32)
    for sides, conditions in (
        ((0, 1), (mem == 0, mem == PEERS - 1)),
        ((2, 3), (at_top, at_low)),
    ):
        for i in sides:
            side_copy(i).start()
        for i in sides:
            side_copy(i).wait()
        if sides[0] == 0:

            @pl.loop(1, PARTS)
            def _(part):
                for i in range(len(ways)):
                    block_copy(part, i).start()

        for i, condition in zip(sides, conditions):

            @pl.when(condition)
            def _(i=i):
                @pl.loop(*((1, SIDE + 1) if i < 2 else (0, SIDE + 2)))
                def _(place):
                    if i < 2:
                        obs_pad[place, 0 if i == 0 else SIDE + 1] = blank
                    else:
                        obs_pad[0 if i == 2 else SIDE + 1, place] = blank

    half_lane = lax.broadcasted_iota(jnp.int32, (1, 128), 1) < HALF
    diagonal = lax.broadcasted_iota(jnp.int32, (HALF, 128), 0) == lax.rem(
        lax.broadcasted_iota(jnp.int32, (HALF, 128), 1), HALF
    )
    pair_eye = jnp.where(diagonal, 1.0, 0.0)
    eye = lax.broadcasted_iota(jnp.int32, (128, 128), 0) == lax.broadcasted_iota(
        jnp.int32, (128, 128), 1
    )
    no_rows = jnp.zeros((HALF, 128), jnp.float32)

    @pl.loop(0, BLOCKS // (2 * PAIRS))
    def _(group):
        start = []
        for pair in range(PAIRS):
            for i in range(2 * NBR):
                place = 2 * pair + i // NBR
                a = group * (PAIRS // 4) + place // SIDE
                b = place % SIDE
                code = neighbour[a, b, i % NBR]
                down_by = lax.div(code, 3)
                right_by = code - 3 * down_by
                block = obs_pad[a + down_by, b + right_by]
                far = (down_by != 1).astype(jnp.int32) + (right_by != 1).astype(jnp.int32)
                weight = jnp.where(
                    far == 0, 1.0, jnp.where(far == 1, side_weight, corner_weight)
                )
                rows_z[pair, i * OBS_MAX : (i + 1) * OBS_MAX, :] = weight * block[:OBS_MAX]
                innov_z[pair, i * OBS_MAX : (i + 1) * OBS_MAX, :] = weight * block[OBS_MAX:]
        rows = [rows_z[pair] for pair in range(PAIRS)]
        grams = [product(z, *split(z.T)) for z in rows]
        smalls = [jnp.where(half_lane, gram[:HALF], gram[HALF:]) for gram in grams]
        traces = [
            jnp.sum(jnp.where(diagonal, small, 0.0), axis=0, keepdims=True) for small in smalls
        ]
        totals = [
            [
                MEMBERS * ridge + jnp.sum(jnp.where(side, trace, 0.0), axis=1, keepdims=True)
                for side in (half_lane, jnp.logical_not(half_lane))
            ]
            for trace in traces
        ]
        for pair, (small, total) in enumerate(zip(smalls, totals)):
            scale = 1.0 / jnp.where(half_lane, total[0], total[1])
            low = ridge * scale
            now_x[pair] = small * scale + low * pair_eye
            now_m[pair] = no_rows
            now_d[pair] = pair_eye
            start.append((low, jnp.ones_like(low)))

        def sweep(_, carry):
            states = [(now_x[i], now_m[i], now_d[i]) for i in range(PAIRS)]
            by_x = [
                pair_product(jnp.concatenate(state, axis=0), state[0]) for state in states
            ]
            factors = [
                0.25 * result[:HALF] - 1.5 * state[0] + 2.25 * pair_eye
                for result, state in zip(by_x, states)
            ]
            by_f = [
                pair_product(jnp.concatenate([x, d], axis=0), factor)
                for (x, _, d), factor in zip(states, factors)
            ]
            ahead = []
            later = []
            for (x, m, d), (low, gain), first, second in zip(states, carry, by_x, by_f):
                new_d = (
                    second[HALF:]
                    + (0.25 * low) * first[2 * HALF :]
                    + (0.25 * low * (low - 6.0)) * d
                )
                new_m = 1.5 * m - 0.5 * first[HALF : 2 * HALF] - (0.5 * gain) * d
                later.append((second[:HALF], new_m, new_d))
                shrink = 1.5 - 0.5 * low
                ahead.append((low * shrink * shrink, gain * shrink))
            for i in range(PAIRS):
                now_x[i], now_m[i], now_d[i] = later[i]
            return tuple(ahead)

        last_low = lax.fori_loop(0, NS_ITERS - 1, sweep, tuple(start))
        states = [(now_x[i], now_m[i], now_d[i]) for i in range(PAIRS)]
        rows = [rows_z[pair] for pair in range(PAIRS)]
        by_x = [pair_product(m, x) for x, m, _ in states]
        ends = []
        for (_, m, d), (_, gain), total, result in zip(states, last_low, totals, by_x):
            both = jnp.where(half_lane, total[0], total[1])
            m = 1.5 * m - 0.5 * result - (0.5 * gain) * d
            m = m * (1.0 / (both * jnp.sqrt(both)))
            ends.append(
                jnp.concatenate(
                    [jnp.where(half_lane, m, 0.0), jnp.where(half_lane, 0.0, m)], axis=0
                )
            )
        by_z = [product(end, *split(z)) for end, z in zip(ends, rows)]
        wide_z = [
            jnp.concatenate(
                [
                    jnp.concatenate([m_z[:HALF], no_rows], axis=0),
                    jnp.concatenate([no_rows, m_z[HALF:]], axis=0),
                ],
                axis=1,
            )
            for m_z in by_z
        ]
        roots_both = [product(z.T, *split(right)) for z, right in zip(rows, wide_z)]
        gains = []
        pulls = []
        for pair, (z, total) in enumerate(zip(rows, totals)):
            for side in range(2):
                low = ridge / total[side]
                gain = 1.0 / jnp.sqrt(total[side])
                for _ in range(NS_ITERS):
                    shrink = 1.5 - 0.5 * low
                    low, gain = low * shrink * shrink, gain * shrink
                gains.append(gain)
                own_rows = slice(side * HALF, side * HALF + HALF)
                pulls.append(
                    jnp.sum(innov_z[pair, own_rows] * z[own_rows], axis=0, keepdims=True)
                )
        for i, (gain, pull) in enumerate(zip(gains, pulls)):
            column = i % 2 * 128
            root = roots_both[i // 2][:, column : column + 128] + jnp.where(eye, gain, 0.0)
            first_pass = jnp.sum(root * pull, axis=1, keepdims=True)
            shift = jnp.sum(root * first_pass, axis=0, keepdims=True)
            weights_now[group * 2 * PAIRS + i] = member_root * root + shift

    flat_lines = lines.reshape(PARTS, 2, MEMBERS * 8, 128)

    def out_copy(part, j):
        return pltpu.make_async_copy(
            lines.at[part, j],
            analysis.at[:, pl.ds(pl.multiple_of(part * 8, 8), 8), pl.ds(j * 128, 128)],
            out_sem.at[part, j],
        )

    own.wait()

    @pl.loop(0, PARTS)
    def _(part):
        for i in range(len(ways)):
            block_copy(part, i).wait()

        @pl.loop(0, 2)
        def _(a):
            places = [part * 2 * SIDE + a * SIDE + b for b in range(SIDE)]
            fields = [gathered[place] for place in places]
            centres = [jnp.mean(field, axis=0, keepdims=True) for field in fields]
            updated = [
                product(weights_now[place], *split(field - centre)) + centre
                for place, field, centre in zip(places, fields, centres)
            ]
            for j in range(2):
                for m in range(MEMBERS // 8):
                    rows = swap_groups(
                        [block[m * 8 : m * 8 + 8] for block in updated[4 * j : 4 * j + 4]]
                    )
                    for r in range(BR):
                        at = pl.ds(m * 64 + a * BR + r, 8, stride=8)
                        flat_lines[part, j, at, :] = rows[r]

        for j in range(2):
            out_copy(part, j).start()

    @pl.loop(0, PARTS)
    def _(part):
        for j in range(2):
            out_copy(part, j).wait()

    store_c.wait()


def assimilate(*arguments):
    field = (ROWS, COLS)
    f32 = jnp.float32
    anywhere = pl.BlockSpec(memory_space=pl.ANY)
    local = pl.BlockSpec(memory_space=pltpu.VMEM)
    halo = pltpu.VMEM((STEPS, TILES, OWN, 128), f32)
    dma = pltpu.SemaphoreType.DMA
    square = pltpu.VMEM((BLOCKS, MEMBERS, 128), f32)
    return pl.pallas_call(
        assimilate_kernel,
        out_shape=(
            jax.ShapeDtypeStruct((MEMBERS, ROWS, 2 * 128), f32),
            jax.ShapeDtypeStruct((OWN, ROWS, COLS), f32),
        ),
        in_specs=[anywhere] * 6 + [local] * 4 + [pl.BlockSpec(memory_space=pltpu.SMEM)],
        out_specs=[anywhere] * 2,
        scratch_shapes=[
            *[pltpu.VMEM((TILES + 2, OWN, PAD_ROWS, 128), f32)] * 2,
            *[pltpu.VMEM((OWN, ROWS, COLS), f32)] * 2,
            *[pltpu.VMEM(field, f32)] * 4,
            *[pltpu.VMEM((8, COLS), f32)] * 2,
            *[pltpu.VMEM(field, f32)] * 5,
            *[halo] * 4,
            pltpu.VMEM((PEERS, BLOCKS, OWN, 128), f32),
            pltpu.VMEM((SIDE, 128), jnp.int32),
            *[pltpu.VMEM((SIDE, 128), f32)] * 2,
            pltpu.VMEM((PEERS, SIDE, 128), jnp.int32),
            pltpu.VMEM((PEERS, SIDE, OWN, 128), f32),
            pltpu.VMEM((SIDE, MEMBERS, 128), f32),
            pltpu.VMEM((SIDE + 2, SIDE + 2, 2 * OBS_MAX, 128), f32),
            *[pltpu.VMEM((PAIRS, 2 * HALF, 128), f32)] * 2,
            *[pltpu.VMEM((PAIRS, HALF, 128), f32)] * 3,
            square, square,
            pltpu.VMEM((PARTS, 2, MEMBERS, 8, 128), f32),
            dma((5,)), dma((TILES,)), dma((2,)), dma((2,)),
            dma((STEPS, 2)), dma((STEPS, 2)), dma((PARTS, PEERS)), dma((PARTS, PEERS)),
            dma((2,)), dma,
            dma((PEERS,)), dma((PEERS,)), dma((PEERS,)), dma((PEERS,)), dma((4,)), dma((4,)),
            dma((PARTS, 2)),
        ],
        compiler_params=pltpu.CompilerParams(
            collective_id=0, has_side_effects=True, vmem_limit_bytes=62 << 20
        ),
        name="assimilate",
    )(*arguments)


def solution(mesh):
    placed = (
        P("mem", "slab", None),
        P("mem", "slab", None),
        P("slab", None),
        P("slab", None),
        P("slab", None),
        P("slab", None),
        P("slab", "mem", None),
        P("slab", "mem", None),
        P("slab", "mem", None),
        P("slab", "mem"),
        P("slab", "mem", None),
    )
    return jax.shard_map(
        assimilate,
        mesh=mesh,
        in_specs=placed,
        out_specs=(P(None, "slab", "mem"), P("mem", "slab", None)),
        check_vma=False,
    )
```

profile of v0, /device:TPU:24, one launch (start us, length us, event | category | flops | bytes accessed | tf_op | source)
XLA Modules:
  0.0 116.6 jit_solution(12425154268799522291)
XLA Ops:
  0.6 1.4 %copy.13.neighbour = s32[8,8,4]{2,1,0:T(8,128)} copy(s32[8,8,4]{1,2,0:T(4,128)} %param.21) | data formatting | bytes 2048 | tf_op args[10]
  2.1 107.5 %assimilate.1 = (f32[128,32,256]{2,1,0:T(8,128)}, f32[8,32,4096]{2,1,0:T(8,128)}) custom-call(f32[8,32,4096]{2,1,0:T(8,128)} %p_in.1, f32[8,32,4096]{2,1,0:T(8,128)} %c_in.1, f32[32,4096]{1,0:T(8,128)} %d_in.1, f32[32,4096]{1,0:T(8,128)} %lp_in.1, f32[32,4096]{1,0:T(8,128)} %lv_in.1, f32[32,4096]{1,0:T(8,128)} %rate_in.1, s32[8,8,16]{2,1,0:T(8,128)} %cell_in.1, ...), custom_call_target="tpu_custom_call" | custom-call | tf_op jit(solution)/shard_map/assimilate/pallas_call | solution.py:606
  109.6 0.0 copy-start
  109.6 4.9 %copy.16 = f32[128,32,256]{2,1,0:T(8,128)} copy(f32[128,32,256]{2,1,0:T(8,128)} %get-tuple-element.4) | data formatting | bytes 8388608
  114.6 0.0 copy-done
  114.6 2.0 %copy.17 = f32[8,32,4096]{2,1,0:T(8,128)} copy(f32[8,32,4096]{2,1,0:T(8,128)S(1)} %copy-done) | data formatting | bytes 8388608
Async XLA Ops:
  109.6 5.0 %copy-start = (f32[8,32,4096]{2,1,0:T(8,128)S(1)}, f32[8,32,4096]{2,1,0:T(8,128)}, u32[]{:S(2)}) copy-start(f32[8,32,4096]{2,1,0:T(8,128)} %get-tuple-element.5) | copy-start | bytes 12582916
where the time goes:
time: 117 us
  Pallas kernels  108 us (92%)
  local copies, waits for them, and re-layouts  8.4 us (7%)
    pallas_call x1, Pallas kernels, assimilate(): pl.pallas_call(assimilate_kernel, out_shape=(jax.ShapeDtypeStruct((MEMBER...  108 us
    unnamed x5, local copies, waits for them, and re-layouts  8.4 us

commit v1 on v0

--- a/solution.py
+++ b/solution.py
@@ -202,23 +202,32 @@
         field.reshape(TILES + 2, OWN * PAD_ROWS, 128) for field in (p, p_other)
     )
 
-    def send_halo(step, source):
-
-        @pl.loop(0, TILES)
-        def _(tile):
-            out_up[step, tile] = source[tile + 1, pl.ds(8, OWN, stride=PAD_ROWS), :]
-            out_down[step, tile] = source[
-                tile + 1, pl.ds(7 + ROWS, OWN, stride=PAD_ROWS), :
-            ]
-
+    def send_halo(step):
         for i in range(2):
             halo_copy(step, i).start()
+
+    first_row = pl.ds(8, OWN, stride=PAD_ROWS)
+    last_row = pl.ds(7 + ROWS, OWN, stride=PAD_ROWS)
+
+    def clear_outside(field, tile):
+        field[tile + 1, pl.ds(7, OWN, stride=PAD_ROWS), :] = zero
+        field[tile + 1, pl.ds(8 + ROWS, OWN, stride=PAD_ROWS), :] = zero
+
+    @pl.loop(0, TILES, unroll=8)
+    def _(tile):
+        clear_outside(flat_other, tile)
 
     @pl.loop(0, TILES)
     def _(tile):
         load_p(tile).wait()
 
-    send_halo(0, flat)
+    @pl.loop(0, TILES, unroll=8)
+    def _(tile):
+        clear_outside(flat, tile)
+        out_up[0, tile] = flat[tile + 1, first_row, :]
+        out_down[0, tile] = flat[tile + 1, last_row, :]
+
+    send_halo(0)
 
     for load in loads:
         load.wait()
@@ -228,7 +237,7 @@
     first, last = lane == 0, lane == 127
     at_top, at_low = slab == 0, slab == SLABS - 1
 
-    @pl.loop(0, TILES)
+    @pl.loop(0, TILES, unroll=4)
     def _(tile):
         here = pl.ds(pl.multiple_of(tile * 128, 128), 128)
         left = pl.ds(pl.multiple_of(jnp.maximum(tile - 1, 0) * 128, 128), 128)
@@ -254,11 +263,11 @@
 
     wide = 4
 
-    def advance(now, content_now, later, content_later, row_tiles):
+    def advance(now, content_now, later, content_later):
 
         @pl.loop(0, TILES // wide)
         def _(group):
-            for row_tile in row_tiles:
+            for row_tile in range(ROWS // 8):
                 rows = slice(row_tile * 8, row_tile * 8 + 8)
                 base = 8 + row_tile * 8
                 heres = [
@@ -291,28 +300,32 @@
                         )
                         content_later[m, rows, heres[j]] = content - release
 
-    def one_step(step, now, content_now, later, content_later, flat_now, flat_later, more):
-        advance(now, content_now, later, content_later, (1, 2))
+    def one_step(step, now, content_now, later, content_later, flat_later, more):
+        advance(now, content_now, later, content_later)
         for i in range(2):
             halo_copy(step, i).wait()
-
-        @pl.loop(0, TILES)
+        following = lax.rem(step + 1, STEPS)
+
+        @pl.loop(0, TILES, unroll=8)
         def _(tile):
-            top = jnp.where(at_top, 0.0, in_top[step, tile])
-            low = jnp.where(at_low, 0.0, in_low[step, tile])
-            flat_now[tile + 1, pl.ds(7, OWN, stride=PAD_ROWS), :] = top
-            flat_now[tile + 1, pl.ds(8 + ROWS, OWN, stride=PAD_ROWS), :] = low
-
-        advance(now, content_now, later, content_later, (0, 3))
+            here = pl.ds(pl.multiple_of(tile * 128, 128), 128)
+            top = jnp.where(at_top, 0.0, in_top[step, tile]) * k_up[0:1, here]
+            low = jnp.where(at_low, 0.0, in_low[step, tile]) * k_down[ROWS - 1 : ROWS, here]
+            top = flat_later[tile + 1, first_row, :] + top
+            low = flat_later[tile + 1, last_row, :] + low
+            flat_later[tile + 1, first_row, :] = top
+            flat_later[tile + 1, last_row, :] = low
+            out_up[following, tile] = top
+            out_down[following, tile] = low
 
         @pl.when(more)
         def _():
-            send_halo(step + 1, flat_later)
+            send_halo(step + 1)
 
     @pl.loop(0, STEPS // 2)
     def _(pair):
-        one_step(2 * pair, p, c, p_other, c_other, flat, flat_other, True)
-        one_step(2 * pair + 1, p_other, c_other, p, c, flat_other, flat, pair < STEPS // 2 - 1)
+        one_step(2 * pair, p, c, p_other, c_other, flat_other, True)
+        one_step(2 * pair + 1, p_other, c_other, p, c, flat, pair < STEPS // 2 - 1)
 
     store_c = pltpu.make_async_copy(c, c_out, c_sem)
     store_c.start()
@@ -339,8 +352,11 @@
 
     mine = pl.ds(pl.multiple_of(mem * OWN, OWN), OWN)
 
+    def place_of(code):
+        return lax.rem(mem // 4 + code // 4, 4) * 4 + lax.rem(mem + code, 4)
+
     def obs_copy(i):
-        target = lax.rem(mem + i, PEERS)
+        target = place_of(i)
         return pltpu.make_async_remote_copy(
             src_ref=obs_send.at[target], dst_ref=obs_in.at[:, mine, :],
             send_sem=obs_send_sem.at[i], recv_sem=obs_recv_sem.at[i],
@@ -348,8 +364,7 @@
         )
 
     def block_copy(part, i):
-        way = ways[i]
-        target = lax.rem(mem // 4 + way[0], 4) * 4 + lax.rem(mem + way[1], 4)
+        target = place_of(i)
         blocks = pl.ds(part * 2 * SIDE, 2 * SIDE)
         return pltpu.make_async_remote_copy(
             src_ref=send.at[target, blocks], dst_ref=gathered.at[blocks, mine, :],
@@ -359,12 +374,12 @@
 
     @pl.loop(1, PEERS)
     def _(i):
-        to_blocks(lax.rem(mem + i, PEERS))
-        obs_copy(i).start()
+        code = lax.rem(7 * i, PEERS)
+        to_blocks(place_of(code))
+        obs_copy(code).start()
+        block_copy(0, code).start()
 
     to_blocks(mem)
-    for i in range(len(ways)):
-        block_copy(0, i).start()
     own = pltpu.make_async_copy(send.at[mem], gathered.at[:, mine, :], own_sem.at[0])
     own.start()
     own_obs = pltpu.make_async_copy(obs_send.at[mem], obs_in.at[:, mine, :], own_sem.at[1])
@@ -411,8 +426,8 @@
 
             @pl.loop(1, PARTS)
             def _(part):
-                for i in range(len(ways)):
-                    block_copy(part, i).start()
+                for way in ways:
+                    block_copy(part, 4 * way[0] + way[1]).start()
 
         for i, condition in zip(sides, conditions):
 
@@ -563,7 +578,8 @@
 
     @pl.loop(0, PARTS)
     def _(part):
-        for i in range(len(ways)):
+        @pl.loop(1, PEERS)
+        def _(i):
             block_copy(part, i).wait()
 
         @pl.loop(0, 2)

time: 117 us -> 109 us (0.932); the launches traced: 117 us -> 107 us
  Pallas kernels: 108 us -> 97.7 us
    pallas_call x1, Pallas kernels: 108 us -> 97.7 us  [assimilate(): pl.pallas_call(assimilate_kernel, out_shape=(jax.ShapeDtypeStruct((MEMBER...]
where the time goes in v1:
time: 109 us; the launch traced here: 107 us
  Pallas kernels  97.7 us (90%)
  local copies, waits for them, and re-layouts  8.4 us (8%)
    pallas_call x1, Pallas kernels, assimilate(): pl.pallas_call(assimilate_kernel, out_shape=(jax.ShapeDtypeStruct((MEMBER...  97.7 us
    unnamed x5, local copies, waits for them, and re-layouts  8.4 us

profile of v1, /device:TPU:24, one launch (start us, length us, event | category | flops | bytes accessed | tf_op | source)
XLA Modules:
  0.0 106.7 jit_solution(10088233264747384481)
XLA Ops:
  0.6 1.4 %copy.13.neighbour = s32[8,8,4]{2,1,0:T(8,128)} copy(s32[8,8,4]{1,2,0:T(4,128)} %param.21) | data formatting | bytes 2048 | tf_op args[10]
  2.1 97.7 %assimilate.1 = (f32[128,32,256]{2,1,0:T(8,128)}, f32[8,32,4096]{2,1,0:T(8,128)}) custom-call(f32[8,32,4096]{2,1,0:T(8,128)} %p_in.1, f32[8,32,4096]{2,1,0:T(8,128)} %c_in.1, f32[32,4096]{1,0:T(8,128)} %d_in.1, f32[32,4096]{1,0:T(8,128)} %lp_in.1, f32[32,4096]{1,0:T(8,128)} %lv_in.1, f32[32,4096]{1,0:T(8,128)} %rate_in.1, s32[8,8,16]{2,1,0:T(8,128)} %cell_in.1, ...), custom_call_target="tpu_custom_call" | custom-call | tf_op jit(solution)/shard_map/assimilate/pallas_call | solution.py:622
  99.8 0.0 copy-start
  99.8 4.9 %copy.16 = f32[128,32,256]{2,1,0:T(8,128)} copy(f32[128,32,256]{2,1,0:T(8,128)} %get-tuple-element.4) | data formatting | bytes 8388608
  104.7 0.0 copy-done
  104.7 2.0 %copy.17 = f32[8,32,4096]{2,1,0:T(8,128)} copy(f32[8,32,4096]{2,1,0:T(8,128)S(1)} %copy-done) | data formatting | bytes 8388608
Async XLA Ops:
  99.8 5.0 %copy-start = (f32[8,32,4096]{2,1,0:T(8,128)S(1)}, f32[8,32,4096]{2,1,0:T(8,128)}, u32[]{:S(2)}) copy-start(f32[8,32,4096]{2,1,0:T(8,128)} %get-tuple-element.5) | copy-start | bytes 12582916

commit v2 on v1

--- a/solution.py
+++ b/solution.py
@@ -36,8 +36,8 @@
 mesh_ids = pl.DeviceIdType.MESH
 
 ways = (
-    (1, 0), (3, 0), (2, 2), (0, 2), (2, 0), (1, 1), (3, 3), (1, 3), (3, 1), (2, 1), (1, 2),
-    (2, 3), (3, 2), (0, 1), (0, 3),
+    (2, 2), (0, 1), (1, 0), (1, 1), (3, 3), (0, 3), (3, 0), (1, 3), (3, 1), (0, 2), (2, 0),
+    (2, 1), (1, 2), (2, 3), (3, 2),
 )
 
 
@@ -458,7 +458,7 @@
                 place = 2 * pair + i // NBR
                 a = group * (PAIRS // 4) + place // SIDE
                 b = place % SIDE
-                code = neighbour[a, b, i % NBR]
+                code = neighbour[a, i % NBR, b]
                 down_by = lax.div(code, 3)
                 right_by = code - 3 * down_by
                 block = obs_pad[a + down_by, b + right_by]
@@ -658,6 +658,10 @@
     )(*arguments)
 
 
+def on_device(*arguments):
+    return assimilate(*arguments[:-1], arguments[-1].transpose(0, 2, 1))
+
+
 def solution(mesh):
     placed = (
         P("mem", "slab", None),
@@ -673,7 +677,7 @@
         P("slab", "mem", None),
     )
     return jax.shard_map(
-        assimilate,
+        on_device,
         mesh=mesh,
         in_specs=placed,
         out_specs=(P(None, "slab", "mem"), P("mem", "slab", None)),

time: 109 us -> 106 us (0.972); the launches traced: 107 us -> 105 us
  local copies, waits for them, and re-layouts: 8.4 us -> 6.96 us
    unnamed x5 -> x4, local copies, waits for them, and re-layouts: 8.4 us -> 6.96 us
where the time goes in v2:
time: 106 us; the launch traced here: 105 us
  Pallas kernels  97.7 us (92%)
  local copies, waits for them, and re-layouts  6.96 us (7%)
    pallas_call x1, Pallas kernels, assimilate(): pl.pallas_call(assimilate_kernel, out_shape=(jax.ShapeDtypeStruct((MEMBER...  97.7 us
    unnamed x4, local copies, waits for them, and re-layouts  6.96 us

profile of v2, /device:TPU:24, one launch (start us, length us, event | category | flops | bytes accessed | tf_op | source)
XLA Modules:
  0.0 105.3 jit_solution(5311646193838972925)
XLA Ops:
  0.6 97.7 %assimilate.1 = (f32[128,32,256]{2,1,0:T(8,128)}, f32[8,32,4096]{2,1,0:T(8,128)}) custom-call(f32[8,32,4096]{2,1,0:T(8,128)} %p_in.1, f32[8,32,4096]{2,1,0:T(8,128)} %c_in.1, f32[32,4096]{1,0:T(8,128)} %d_in.1, f32[32,4096]{1,0:T(8,128)} %lp_in.1, f32[32,4096]{1,0:T(8,128)} %lv_in.1, f32[32,4096]{1,0:T(8,128)} %rate_in.1, s32[8,8,16]{2,1,0:T(8,128)} %cell_in.1, ...), custom_call_target="tpu_custom_call" | custom-call | tf_op jit(solution)/shard_map/assimilate/pallas_call | solution.py:622
  98.3 0.0 copy-start
  98.3 4.9 %copy.15 = f32[128,32,256]{2,1,0:T(8,128)} copy(f32[128,32,256]{2,1,0:T(8,128)} %get-tuple-element.4) | data formatting | bytes 8388608
  103.2 0.0 copy-done
  103.2 2.0 %copy.16 = f32[8,32,4096]{2,1,0:T(8,128)} copy(f32[8,32,4096]{2,1,0:T(8,128)S(1)} %copy-done) | data formatting | bytes 8388608
Async XLA Ops:
  98.3 5.0 %copy-start = (f32[8,32,4096]{2,1,0:T(8,128)S(1)}, f32[8,32,4096]{2,1,0:T(8,128)}, u32[]{:S(2)}) copy-start(f32[8,32,4096]{2,1,0:T(8,128)} %get-tuple-element.5) | copy-start | bytes 12582916

commit v3 on v2

--- a/solution.py
+++ b/solution.py
@@ -122,6 +122,20 @@
     for load in loads[1:]:
         load.start()
 
+    barrier = pltpu.get_barrier_semaphore()
+
+    @pl.loop(1, PEERS)
+    def _(i):
+        pl.semaphore_signal(
+            barrier, inc=1, device_id=(lax.rem(mem + i, PEERS), slab),
+            device_id_type=pl.DeviceIdType.MESH,
+        )
+
+    for other in (above, below):
+        pl.semaphore_signal(
+            barrier, inc=1, device_id=(mem, other), device_id_type=pl.DeviceIdType.MESH
+        )
+
     lane = lax.broadcasted_iota(jnp.int32, (8, 128), 1)
     line = lax.broadcasted_iota(jnp.int32, (8, 128), 0)
     slot_group = lane // OBS_MAX
@@ -140,20 +154,6 @@
     counts = lay_out(lambda b: jnp.broadcast_to(count_in[:, b : b + 1], (SIDE, 128)))
     live = lax.rem(lane, OBS_MAX) < counts
     roots[...] = jnp.where(live, jnp.sqrt(slots_of(error_in)), 0.0)
-
-    barrier = pltpu.get_barrier_semaphore()
-
-    @pl.loop(1, PEERS)
-    def _(i):
-        pl.semaphore_signal(
-            barrier, inc=1, device_id=(lax.rem(mem + i, PEERS), slab),
-            device_id_type=pl.DeviceIdType.MESH,
-        )
-
-    for other in (above, below):
-        pl.semaphore_signal(
-            barrier, inc=1, device_id=(mem, other), device_id_type=pl.DeviceIdType.MESH
-        )
 
     zero = jnp.zeros((8, 128), jnp.float32)
     for field in (p, p_other):

time: 106 us -> 106 us (level)
  no operation moved by 1% of the time
where the time goes in v3:
time: 106 us; the launch traced here: 105 us
  Pallas kernels  97.4 us (92%)
  local copies, waits for them, and re-layouts  6.96 us (7%)
    pallas_call x1, Pallas kernels, assimilate(): pl.pallas_call(assimilate_kernel, out_shape=(jax.ShapeDtypeStruct((MEMBER...  97.4 us
    unnamed x4, local copies, waits for them, and re-layouts  6.96 us

profile of v3, /device:TPU:24, one launch (start us, length us, event | category | flops | bytes accessed | tf_op | source)
XLA Modules:
  0.0 105.0 jit_solution(7774054991286724842)
XLA Ops:
  0.6 97.4 %assimilate.1 = (f32[128,32,256]{2,1,0:T(8,128)}, f32[8,32,4096]{2,1,0:T(8,128)}) custom-call(f32[8,32,4096]{2,1,0:T(8,128)} %p_in.1, f32[8,32,4096]{2,1,0:T(8,128)} %c_in.1, f32[32,4096]{1,0:T(8,128)} %d_in.1, f32[32,4096]{1,0:T(8,128)} %lp_in.1, f32[32,4096]{1,0:T(8,128)} %lv_in.1, f32[32,4096]{1,0:T(8,128)} %rate_in.1, s32[8,8,16]{2,1,0:T(8,128)} %cell_in.1, ...), custom_call_target="tpu_custom_call" | custom-call | tf_op jit(solution)/shard_map/assimilate/pallas_call | solution.py:622
  98.0 0.0 copy-start
  98.1 4.9 %copy.15 = f32[128,32,256]{2,1,0:T(8,128)} copy(f32[128,32,256]{2,1,0:T(8,128)} %get-tuple-element.4) | data formatting | bytes 8388608
  103.0 0.0 copy-done
  103.0 2.0 %copy.16 = f32[8,32,4096]{2,1,0:T(8,128)} copy(f32[8,32,4096]{2,1,0:T(8,128)S(1)} %copy-done) | data formatting | bytes 8388608
Async XLA Ops:
  98.0 5.0 %copy-start = (f32[8,32,4096]{2,1,0:T(8,128)S(1)}, f32[8,32,4096]{2,1,0:T(8,128)}, u32[]{:S(2)}) copy-start(f32[8,32,4096]{2,1,0:T(8,128)} %get-tuple-element.5) | copy-start | bytes 12582916

commit v4 on v3

--- a/solution.py
+++ b/solution.py
@@ -112,15 +112,14 @@
             ((d_in, dif), (lp_in, lp), (lv_in, lv), (rate_in, rate), (c_in, c))
         )
     ]
-    for load in loads[:1]:
+    for load in loads[:-1]:
         load.start()
 
     @pl.loop(0, TILES)
     def _(tile):
         load_p(tile).start()
 
-    for load in loads[1:]:
-        load.start()
+    loads[-1].start()
 
     barrier = pltpu.get_barrier_semaphore()
 
@@ -217,19 +216,7 @@
     def _(tile):
         clear_outside(flat_other, tile)
 
-    @pl.loop(0, TILES)
-    def _(tile):
-        load_p(tile).wait()
-
-    @pl.loop(0, TILES, unroll=8)
-    def _(tile):
-        clear_outside(flat, tile)
-        out_up[0, tile] = flat[tile + 1, first_row, :]
-        out_down[0, tile] = flat[tile + 1, last_row, :]
-
-    send_halo(0)
-
-    for load in loads:
+    for load in loads[:-1]:
         load.wait()
     for copy in dif_copies:
         copy.wait()
@@ -260,6 +247,20 @@
                 ref[rows, here] = side
             keep[rows, here] = 1.0 - ((sides[0] + sides[1]) + (sides[2] + sides[3]))
             lv[rows, here] = lv[rows, here] * rate[rows, here]
+
+    @pl.loop(0, TILES)
+    def _(tile):
+        load_p(tile).wait()
+
+    @pl.loop(0, TILES, unroll=8)
+    def _(tile):
+        clear_outside(flat, tile)
+        out_up[0, tile] = flat[tile + 1, first_row, :]
+        out_down[0, tile] = flat[tile + 1, last_row, :]
+
+    send_halo(0)
+
+    loads[-1].wait()
 
     wide = 4
 

time: 106 us -> 107 us (level)
  no operation moved by 1% of the time
where the time goes in v4:
time: 107 us; the launch traced here: 105 us
  Pallas kernels  97.8 us (91%)
  local copies, waits for them, and re-layouts  6.96 us (7%)
    pallas_call x1, Pallas kernels, assimilate(): pl.pallas_call(assimilate_kernel, out_shape=(jax.ShapeDtypeStruct((MEMBER...  97.8 us
    unnamed x4, local copies, waits for them, and re-layouts  6.96 us

profile of v4, /device:TPU:24, one launch (start us, length us, event | category | flops | bytes accessed | tf_op | source)
XLA Modules:
  0.0 105.4 jit_solution(11586503890865667625)
XLA Ops:
  0.6 97.8 %assimilate.1 = (f32[128,32,256]{2,1,0:T(8,128)}, f32[8,32,4096]{2,1,0:T(8,128)}) custom-call(f32[8,32,4096]{2,1,0:T(8,128)} %p_in.1, f32[8,32,4096]{2,1,0:T(8,128)} %c_in.1, f32[32,4096]{1,0:T(8,128)} %d_in.1, f32[32,4096]{1,0:T(8,128)} %lp_in.1, f32[32,4096]{1,0:T(8,128)} %lv_in.1, f32[32,4096]{1,0:T(8,128)} %rate_in.1, s32[8,8,16]{2,1,0:T(8,128)} %cell_in.1, ...), custom_call_target="tpu_custom_call" | custom-call | tf_op jit(solution)/shard_map/assimilate/pallas_call | solution.py:623
  98.5 0.0 copy-start
  98.5 4.9 %copy.15 = f32[128,32,256]{2,1,0:T(8,128)} copy(f32[128,32,256]{2,1,0:T(8,128)} %get-tuple-element.4) | data formatting | bytes 8388608
  103.4 0.0 copy-done
  103.4 2.0 %copy.16 = f32[8,32,4096]{2,1,0:T(8,128)} copy(f32[8,32,4096]{2,1,0:T(8,128)S(1)} %copy-done) | data formatting | bytes 8388608
Async XLA Ops:
  98.5 5.0 %copy-start = (f32[8,32,4096]{2,1,0:T(8,128)S(1)}, f32[8,32,4096]{2,1,0:T(8,128)}, u32[]{:S(2)}) copy-start(f32[8,32,4096]{2,1,0:T(8,128)} %get-tuple-element.5) | copy-start | bytes 12582916
